TPU v7x, 32 devices: a whole 2x2x4 slice. The times are simulated.
32 devices in a mesh: row: 8 (over y, x, core), rhs: 4 (over z).
Axes of the slice: x: 2, y: 2, z: 4, core: 2. Of those that a mesh axis runs over, the one named last changes fastest.
Arguments:
- right_sides: float32 [16384, 4096], P('row', 'rhs'), may hold values from -6 to 6
- panel_diag: float32 [2, 512, 512], replicated, as said below
- left_factor: bfloat16 [16384, 2, 512], P('row', None, 'rhs'), may hold values from -0.25 to 0.25
- right_factor: bfloat16 [16384, 2, 512], P('row', None, 'rhs'), may hold values from -0.25 to 0.25
- tile_scale: float32 [32, 2], P('row'), may hold values from 0.3 to 1.5
- tile_rank: int32 [32, 2], P('row'), may hold values from 128 to 512, as said below
Outputs:
- solved: float32 [16384, 4096], P('row', 'rhs')
Inputs may be any that keep to these rules, and one draw needn't show every extreme that they name: panel_diag[k] is lower triangular with diagonal entries of 1 or more. `tile_rank`: every rank is a multiple of 128; some block has rank 512 in both panels.
All inputs are finite; a program needn't handle non-finite values.
Results may differ from a plain program's by a relative error of at most 0.0003.
Values may be sent and summed in bfloat16 or wider, within the bound.
A program may use at most 128 MiB of HBM per device.

v0:
```python
import jax
import jax.numpy as jnp
from jax import lax
from jax.sharding import PartitionSpec as P


def spread(value, axis, source):
    kept = jnp.where(lax.axis_index(axis) == source, value, 0).astype(value.dtype)
    return lax.psum(kept, axis)


def solve_panel(triangle, target):
    return lax.linalg.triangular_solve(triangle, target, left_side=True, lower=True)


def send_second(solution):
    return spread(solution, "row", 1)


def shards(right_sides, panel_diag, left_factor, right_factor, tile_scale, tile_rank):
    row_count, column_count = right_sides.shape
    panel_rows = panel_diag.shape[1]
    block_count = row_count // panel_rows
    row_index = lax.axis_index("row")
    global_block = jnp.arange(block_count, dtype=jnp.int32) * lax.axis_size("row") + row_index
    columns = jnp.arange(panel_rows, dtype=jnp.int32)
    blocks = right_sides.reshape(block_count, panel_rows, column_count)
    weights = []
    for panel_index in range(2):
        active = jnp.where(global_block > panel_index, tile_scale[:, panel_index], 0.0)
        weights.append(
            active[:, None]
            * (columns[None, :] < tile_rank[:, panel_index : panel_index + 1]).astype(jnp.float32)
        )
    left_full, right_full = (
        lax.all_gather(left_factor, "rhs", axis=2, tiled=True),
        lax.all_gather(right_factor, "rhs", axis=2, tiled=True),
    )
    left_blocks = left_full.reshape(block_count, panel_rows, 2, panel_rows)
    right_blocks = right_full.reshape(block_count, panel_rows, 2, panel_rows)

    def apply_panel(panel_index, solution, current, chosen):
        inner = jnp.einsum(
            "lqr,qn->lrn",
            right_blocks[chosen, :, panel_index, :],
            solution,
            precision=lax.Precision.HIGH,
            preferred_element_type=jnp.float32,
        )
        inner = inner * weights[panel_index][chosen][:, :, None]
        return current[chosen] - jnp.einsum(
            "lpr,lrn->lpn",
            left_blocks[chosen, :, panel_index, :],
            inner,
            precision=lax.Precision.HIGH,
            preferred_element_type=jnp.float32,
        )

    first_local = solve_panel(panel_diag[0], blocks[0])
    first_solution = spread(first_local, "row", 0)
    leading = apply_panel(0, first_solution, blocks, slice(0, 1))
    second_local = solve_panel(panel_diag[1], leading[0])
    second_solution = send_second(second_local)
    trailing = apply_panel(0, first_solution, blocks, slice(1, None))
    blocks = jnp.concatenate([leading, trailing], axis=0)
    blocks = apply_panel(1, second_solution, blocks, slice(None))
    leading_block = jnp.where(
        row_index == 0, first_solution, jnp.where(row_index == 1, second_solution, blocks[0])
    )
    blocks = jnp.concatenate([leading_block[None], blocks[1:]], axis=0)
    return blocks.reshape(row_count, column_count)


def solution(mesh):
    placed = (
        P("row", "rhs"),
        P(),
        P("row", None, "rhs"),
        P("row", None, "rhs"),
        P("row", None),
        P("row", None),
    )
    return jax.shard_map(
        shards, mesh=mesh, in_specs=placed, out_specs=P("row", "rhs"), check_vma=False
    )
```

profile of v0, /device:TPU:7, one launch (start us, length us, event | category | flops | bytes accessed | tf_op | source)
XLA Modules:
  0.0 290.2 jit_solution(15137715391896621521)
XLA Ops:
  7.4 0.7 all-gather.5.cloned.1.call-update
  8.2 1.8 bitcast_select_fusion
  10.0 8.1 %while.4 = (s32[]{:T(128)}, f32[512,512]{1,0:T(8,128)S(1)}, s32[4,2]{0,1:T(2,128)S(1)}, f32[4,128,128]{2,1,0:T(8,128)S(1)}, s32[]{:T(128)}) while((s32[]{:T(128)}, f32[512,512]{1,0:T(8,128)S(1)}, s32[4,2]{0,1:T(2,128)S(1)}, f32[4,128,128]{2,1,0:T(8,128)S(1)}, s32[]{:T(128)}) %tuple.38), condition=%wide.while_cond, body=%wide.while_body.sunk | while | flops 2 | bytes 131189 | solution.py:13
  10.7 1.3 bitcast_dynamic-update-slice_fusion.4
  12.7 1.3 bitcast_dynamic-update-slice_fusion.4
  14.7 1.3 bitcast_dynamic-update-slice_fusion.4
  16.7 1.3 bitcast_dynamic-update-slice_fusion.4
  18.1 39.3 %custom-call.4 = f32[4,128,128]{1,2,0:T(8,128)S(1)} custom-call(f32[4,128,128]{2,1,0:T(8,128)S(1)} %get-tuple-element.20), custom_call_target="InvertDiagBlocksLowerTriangular" | custom-call | tf_op jit(solution)/shard_map/triangular_solve/custom-call.1 | solution.py:13
  57.4 1.7 fusion.51
  59.1 1.6 convolution_subtract_fusion.3
  60.7 0.6 fusion.64
  61.3 1.8 convolution_subtract_fusion.1
  63.1 0.6 fusion.62
  63.7 2.1 fusion.38
  65.9 0.6 fusion.61
  66.5 1.6 maximum_select_fusion
  68.2 1.1 copy-done.6
  69.3 1.1 copy.9
  70.6 0.6 copy-done.8
  71.3 8.1 %while.5 = (s32[]{:T(128)}, f32[512,512]{1,0:T(8,128)S(1)}, s32[4,2]{0,1:T(2,128)S(1)}, f32[4,128,128]{2,1,0:T(8,128)S(1)}, s32[]{:T(128)}) while((s32[]{:T(128)}, f32[512,512]{1,0:T(8,128)S(1)}, s32[4,2]{0,1:T(2,128)S(1)}, f32[4,128,128]{2,1,0:T(8,128)S(1)}, s32[]{:T(128)}) %tuple.52), condition=%wide.while_cond.clone, body=%wide.while_body.clone.sunk | while | flops 2 | bytes 131189 | solution.py:13
  71.4 0.6 fusion.87
  72.0 1.3 bitcast_dynamic-update-slice_fusion.5
  74.0 1.3 bitcast_dynamic-update-slice_fusion.5
  76.1 1.3 bitcast_dynamic-update-slice_fusion.5
  78.1 1.3 bitcast_dynamic-update-slice_fusion.5
  79.5 39.5 %custom-call.5 = f32[4,128,128]{1,2,0:T(8,128)S(1)} custom-call(f32[4,128,128]{2,1,0:T(8,128)S(1)} %get-tuple-element.21), custom_call_target="InvertDiagBlocksLowerTriangular" | custom-call | tf_op jit(solution)/shard_map/triangular_solve/custom-call.1 | solution.py:13
  119.0 5.1 %copy.10 = bf16[2048,2,512]{2,0,1:T(8,128)(2,1)} copy(bf16[2048,2,512]{2,1,0:T(2,128)(2,1)} %all-gather.5.cloned.1.call-done) | data formatting | bytes 8388608 | tf_op jit(solution)/shard_map/all_gather | solution.py:36
  124.1 4.9 %all-reduce.3.cloned.1.call-done = f32[512,1024]{1,0:T(8,128)} async-done(((f32[512,1024]{1,0:T(8,128)}), f32[512,1024]{1,0:T(8,128)}) %all-reduce.3.cloned.1.call-update) | async-done | bytes 2097168 | tf_op jit(solution)/shard_map/psum | solution.py:9
  129.0 49.0 %all-gather.3.cloned.1.call-done = bf16[2048,2,512]{2,0,1:T(8,128)(2,1)} async-done(((bf16[2048,2,128]{2,0,1:T(8,128)(2,1)}), bf16[2048,2,512]{2,0,1:T(8,128)(2,1)}) %all-gather.3.cloned.1.call-update) | async-done | bytes 4194320 | tf_op jit(solution)/shard_map/all_gather | solution.py:37
  178.0 3.0 %fusion.50 = f32[1024,512]{1,0:T(8,128)S(1)} fusion(f32[512,1024]{1,0:T(8,128)} %all-reduce.3.cloned.1.call-done, bf16[4,512,2,512]{3,1,0,2:T(8,128)(2,1)} %bitcast.126), kind=kOutput, calls=%fused_computation.64 | convolution fusion | flops 1610612736 | bytes 4718592 | tf_op jit(solution)/shard_map/lqr,qn->lrn/dot_general | solution.py:43
  181.0 3.1 %bitcast_subtract_fusion.1 = f32[512,1024]{1,0:T(8,128)S(1)} fusion(f32[2048,1024]{1,0:T(8,128)} %param.8, f32[1024,512]{1,0:T(8,128)S(1)} %fusion.50, f32[512]{0:T(512)S(1)} %bitcast.129, bf16[4,512,2,512]{3,1,0,2:T(8,128)(2,1)} %bitcast.123), kind=kOutput, calls=%fused_computation.27 | convolution fusion | flops 1611661312 | bytes 6817792 | tf_op jit(solution)/shard_map/lpr,lrn->lpn/dot_general | solution.py:51
  184.2 0.6 fusion.48
  185.4 0.6 fusion.60
  186.0 0.7 convolution_subtract_fusion
  186.8 0.6 fusion.58
  187.4 1.1 fusion.35
  188.5 0.6 fusion.57
  189.2 1.6 maximum_select_fusion.1
  190.8 1.6 copy-done.3
  192.3 5.1 %fusion.17 = f32[1024,3,512]{2,0,1:T(8,128)S(1)} fusion(f32[512,1024]{1,0:T(8,128)S(1)} %copy-done.3, bf16[4,512,2,512]{3,1,0,2:T(8,128)(2,1)} %bitcast.127), kind=kOutput, calls=%fused_computation.25 | convolution fusion | flops 4831838208 | bytes 9961472 | tf_op jit(solution)/shard_map/lqr,qn->lrn/dot_general | solution.py:43
  197.5 7.5 %bitcast_subtract_fusion = f32[3,512,1024]{2,1,0:T(8,128)} fusion(f32[3,512,1024]{2,1,0:T(8,128)S(1)} %bitcast.121, f32[1024,3,512]{2,0,1:T(8,128)S(1)} %fusion.17, f32[3,512]{1,0:T(4,128)S(1)} %slice.186, bf16[4,512,2,512]{3,1,0,2:T(8,128)(2,1)} %bitcast.124), kind=kOutput, calls=%fused_computation.9 | convolution fusion | flops 4834983936 | bytes 20453376 | tf_op jit(solution)/shard_map/lpr,lrn->lpn/dot_general | solution.py:51
  204.9 43.1 %all-reduce.5.cloned.1.call-done = f32[512,1024]{1,0:T(8,128)} async-done(((f32[512,1024]{1,0:T(8,128)}), f32[512,1024]{1,0:T(8,128)}) %all-reduce.5.cloned.1.call-update) | async-done | bytes 2097168 | tf_op jit(solution)/shard_map/psum | solution.py:9
  248.0 10.3 %fusion.15 = f32[1024,4,512]{2,0,1:T(8,128)} fusion(bf16[4,512,2,512]{3,1,0,2:T(8,128)(2,1)} %bitcast.128, f32[512,1024]{1,0:T(8,128)} %all-reduce.5.cloned.1.call-done), kind=kOutput, calls=%fused_computation.21 | convolution fusion | flops 6442450944 | bytes 12582912 | tf_op jit(solution)/shard_map/lqr,qn->lrn/dot_general | solution.py:43
  258.3 12.8 %maximum_subtract_fusion = f32[4,512,1024]{2,1,0:T(8,128)} fusion(f32[3,512,1024]{2,1,0:T(8,128)S(1)} %copy-done.1, f32[1,512,1024]{2,1,0:T(8,128)} %bitcast.122, f32[1024,4,512]{2,0,1:T(8,128)} %fusion.15, f32[4,512]{1,0:T(4,128)S(1)} %fusion.66, bf16[4,512,2,512]{3,1,0,2:T(8,128)(2,1)} %bitcast.125), kind=kOutput, calls=%fused_computation.4 | convolution fusion | flops 6448742400 | bytes 27271168 | tf_op jit(solution)/shard_map/lpr,lrn->lpn/dot_general | solution.py:51
  271.1 3.4 %copy-done = f32[4,512,1024]{2,1,0:T(8,128)S(1)} copy-done((f32[4,512,1024]{2,1,0:T(8,128)S(1)}, f32[4,512,1024]{2,1,0:T(8,128)}, u32[]{:S(2)}) %copy-start) | copy-done | bytes 8388632
  275.7 0.7 fusion.14
  276.4 2.1 slice-done
  278.5 4.2 %pad_maximum_fusion = f32[4,512,1024]{2,1,0:T(8,128)} fusion(f32[3,512,1024]{2,1,0:T(8,128)S(1)} %slice-done, f32[1,512,1024]{2,1,0:T(8,128)S(1)} %fusion.14), kind=kLoop, calls=%fused_computation.5 | loop fusion | flops 2097152 | bytes 16777216 | tf_op jit(solution)/shard_map/concatenate | solution.py:70
  (54 shorter events, 7.0 us)
Async XLA Ops:
  7.4 111.7 %all-gather.5.cloned.1.call-start = ((), (), s32[]{:S(2)}) async-start(), calls=%async_computation.2 | async-start | bytes 5242880 | tf_op jit(solution)/shard_map/all_gather | solution.py:36
  8.1 120.9 %all-reduce.3.cloned.1.call-start = ((), (), s32[]{:S(2)}) async-start(), calls=%async_computation | async-start | bytes 4194304 | tf_op jit(solution)/shard_map/psum | solution.py:9
  68.1 1.2 copy-start.6
  68.1 109.9 %all-gather.3.cloned.1.call-start = ((), (), s32[]{:S(2)}) async-start(), calls=%async_computation.1 | async-start | bytes 5242880 | tf_op jit(solution)/shard_map/all_gather | solution.py:37
  70.5 0.7 copy-start.8
  70.5 0.7 copy-start.9
  70.5 177.5 %all-reduce.5.cloned.1.call-start = ((), (), s32[]{:S(2)}) async-start(), calls=%async_computation.3 | async-start | bytes 4194304 | tf_op jit(solution)/shard_map/psum | solution.py:9
  71.3 52.9 %copy-start.7 = (f32[4,512]{1,0:T(4,128)}, f32[4,512]{1,0:T(4,128)S(1)}, u32[]{:S(2)}) copy-start(f32[4,512]{1,0:T(4,128)S(1)} %fusion.65) | copy-start | bytes 24580
  178.0 3.0 %slice-start.2 = ((f32[4,512]{1,0:T(4,128)}), f32[1,512]{1,0:T(1,128)S(1)}, s32[]{:S(2)}) async-start(f32[4,512]{1,0:T(4,128)} %copy-done.7), calls=%async_computation.6 | async-start | bytes 4096 | tf_op jit(solution)/shard_map/slice | solution.py:50
  184.2 3.3 %copy-start.2 = (f32[512,1024]{1,0:T(8,128)}, f32[512,1024]{1,0:T(8,128)S(1)}, u32[]{:S(2)}) copy-start(f32[512,1024]{1,0:T(8,128)S(1)} %bitcast_subtract_fusion.1) | copy-start | bytes 6291460
  190.7 1.6 copy-start.3
  192.3 5.1 %slice-start.1 = ((f32[2048,1024]{1,0:T(8,128)}), f32[1536,1024]{1,0:T(8,128)S(1)}, s32[]{:S(2)}) async-start(f32[2048,1024]{1,0:T(8,128)} %param.8), calls=%async_computation.5 | async-start | bytes 12582912 | tf_op jit(solution)/shard_map/slice | solution.py:51
  248.0 10.3 %copy-start.1 = (f32[3,512,1024]{2,1,0:T(8,128)S(1)}, f32[3,512,1024]{2,1,0:T(8,128)}, u32[]{:S(2)}) copy-start(f32[3,512,1024]{2,1,0:T(8,128)} %bitcast_subtract_fusion) | copy-start | bytes 18874372
  271.1 3.4 %copy-start = (f32[4,512,1024]{2,1,0:T(8,128)S(1)}, f32[4,512,1024]{2,1,0:T(8,128)}, u32[]{:S(2)}) copy-start(f32[4,512,1024]{2,1,0:T(8,128)} %maximum_subtract_fusion) | copy-start | bytes 25165828
  271.1 4.0 %copy-start.4 = (f32[512,1024]{1,0:T(8,128)S(1)}, f32[512,1024]{1,0:T(8,128)}, u32[]{:S(2)}) copy-start(f32[512,1024]{1,0:T(8,128)} %all-reduce.3.cloned.1.call-done) | copy-start | bytes 6291460
  271.1 4.6 %copy-start.5 = (f32[512,1024]{1,0:T(8,128)S(1)}, f32[512,1024]{1,0:T(8,128)}, u32[]{:S(2)}) copy-start(f32[512,1024]{1,0:T(8,128)} %all-reduce.5.cloned.1.call-done) | copy-start | bytes 6291460
  275.7 2.8 slice-start
Sparse Core Ops, SparseCore 0:
  9.7 84.6 all-gather.4
  96.0 81.9 all-gather.2
Sparse Core Ops, SparseCore 1:
  68.2 60.8 all-reduce.2
  190.8 57.1 all-reduce.4
where the time goes:
time: 294 us; the launch traced here: 290 us
  waiting for transfers between devices  97.7 us (33%)
  other arithmetic  88.8 us (30%)
  matrix products  55.9 us (19%)
  local copies, waits for them, and re-layouts  32.3 us (11%)
  between operations  15.1 us (5%)
    another operation x4, other arithmetic, solve_panel(): lax.linalg.triangular_solve(triangle, target, left_side=True, lower=True)  80.6 us
    all_gather x1, waiting for transfers between devices, shards(): lax.all_gather(right_factor, 'rhs', axis=2, tiled=True)  49 us
    psum x2, waiting for transfers between devices, spread(): return lax.psum(kept, axis)  47.9 us
    dot_general x3, matrix products, apply_panel(): jnp.einsum('lpr,lrn->lpn', left_blocks[chosen, :, panel_index, :], inner,...  23.4 us
    dot_general x3, matrix products, apply_panel(): jnp.einsum('lqr,qn->lrn', right_blocks[chosen, :, panel_index, :], soluti...  18.4 us
    another operation x27, local copies, waits for them, and re-layouts, solve_panel(): lax.linalg.triangular_solve(triangle, target, left_side=True, lower=True)  16.1 us
    another operation x14, matrix products, solve_panel(): lax.linalg.triangular_solve(triangle, target, left_side=True, lower=True)  14 us
    unnamed x21, local copies, waits for them, and re-layouts  9.07 us
  transfers between devices with their start and end apart: 4, of which 3 were waited for; matrix products, arithmetic and copies ran while one was open for 44% of the time, Pallas kernels for 0%

commit v1 on v0

v1 whole, which is shorter than its diff:
```python
import functools

import jax
import jax.numpy as jnp
from jax import lax
from jax.experimental import pallas as pl
from jax.experimental.pallas import tpu as pltpu
from jax.sharding import PartitionSpec as P

MESH = pl.DeviceIdType.MESH
HIGHEST = lax.Precision.HIGHEST
BASE = 128


def split(value):
    high = value.astype(jnp.bfloat16)
    return high, (value - high.astype(jnp.float32)).astype(jnp.bfloat16)


def dot(a, b, precision=None):
    return jnp.dot(a, b, preferred_element_type=jnp.float32, precision=precision)


def invert_lower(block):
    size = block.shape[0]
    row = lax.broadcasted_iota(jnp.int32, block.shape, 0)
    column = lax.broadcasted_iota(jnp.int32, block.shape, 1)
    inverse = jnp.where(row == column, 1.0 / jnp.where(row == column, block, 1.0), 0.0)
    width = 1
    while width < size:
        row_part, column_part = row // width, column // width
        coupling = jnp.where(
            (row_part % 2 == 1) & (row_part - 1 == column_part), block, 0.0
        )
        inverse = inverse - dot(inverse, dot(coupling, inverse, HIGHEST), HIGHEST)
        width *= 2
    return inverse


def front_kernel(
    rows, ranks,
    scale, sides, diag, factors, out,
    gathered, held, high, low, solved, inverse,
    own_sem, in_sem, out_sem, send_sem, recv_sem, x_send, x_recv,
):
    row, rank = lax.axis_index("row"), lax.axis_index("rhs")
    tiles = factors.shape[0]
    blocks = tiles // 2
    size = diag.shape[1]
    chunks, chunk = solved.shape[1], solved.shape[4]
    bits = rows.bit_length() - 1

    own_copy = pltpu.make_async_copy(factors, gathered.at[rank], own_sem)
    loads = [
        pltpu.make_async_copy(sides.at[l], held.at[l], in_sem.at[l]) for l in range(blocks)
    ]
    stores = [
        pltpu.make_async_copy(held.at[l], out.at[l], out_sem.at[l]) for l in range(blocks)
    ]
    for load in loads:
        load.start()
    own_copy.start()

    barrier = pltpu.get_barrier_semaphore()
    for step in (1, ranks - 1):
        pl.semaphore_signal(
            barrier, inc=1, device_id=(row, lax.rem(rank + step, ranks)), device_id_type=MESH
        )
    for bit in range(bits):
        pl.semaphore_signal(
            barrier, inc=1, device_id=(row ^ (1 << bit), rank), device_id_type=MESH
        )
    pl.semaphore_wait(barrier, 2 + bits)

    def relay(side, tile, hop, own=False):
        step = 1 if side == 0 else -1
        origin = lax.rem(rank - step * hop + 2 * ranks, ranks)
        target = lax.rem(rank + step + ranks, ranks)
        return pltpu.make_async_remote_copy(
            src_ref=factors.at[tile] if hop == 0 else gathered.at[origin, tile],
            dst_ref=gathered.at[origin, tile],
            send_sem=send_sem.at[side, tile, hop],
            recv_sem=recv_sem.at[side, tile, hop],
            device_id=(row, target),
            device_id_type=MESH,
        )

    def sends(side, hop):
        if side == 0:
            return (rank >= hop) & (rank + 1 < ranks)
        return (rank + hop < ranks) & (rank >= 1)

    def receives(side, hop):
        return rank >= hop + 1 if side == 0 else rank + hop + 1 < ranks

    def start_relay(side, tile, hop):
        @pl.when(sends(side, hop))
        def _():
            relay(side, tile, hop).start()

    def wait_relay(side, tile, hop):
        @pl.when(receives(side, hop))
        def _():
            relay(side, tile, hop).wait_recv()

    def pass_on(panel, part, bit):
        return pltpu.make_async_remote_copy(
            src_ref=solved.at[panel, part],
            dst_ref=solved.at[panel, part],
            send_sem=x_send.at[panel, part, bit],
            recv_sem=x_recv.at[panel, part],
            device_id=(row ^ (1 << bit), rank),
            device_id_type=MESH,
        )

    def pass_down(panel, part, start=True):
        relative = row ^ panel
        for bit in range(bits):
            @pl.when(lax.rem(relative, 2 << bit) == 0)
            def _():
                copy = pass_on(panel, part, bit)
                if start:
                    copy.start()
                else:
                    copy.wait_send()

    def take_solution(panel):
        @pl.when(row != panel)
        def _():
            for part in range(chunks):
                pass_on(panel, part, 0).wait_recv()
                pass_down(panel, part)

    def product(tile, panel, part):
        a, b = high[tile], low[tile]
        x, y = solved[panel, part, 0], solved[panel, part, 1]
        return dot(a, x) + (dot(b, x) + dot(a, y))

    def prepare(panel):
        for i in range(size // BASE):
            span = pl.ds(i * BASE, BASE)
            inverse[i] = invert_lower(diag[panel, span, span])

    def solve(panel):
        for part in range(chunks):
            columns = pl.ds(part * chunk, chunk)
            for i in range(size // BASE):
                span = pl.ds(i * BASE, BASE)
                value = held[0, span, columns]
                if i:
                    value = value - dot(
                        diag[panel, span, pl.ds(0, i * BASE)],
                        held[0, pl.ds(0, i * BASE), columns],
                        HIGHEST,
                    )
                value = dot(inverse[i], value, HIGHEST)
                held[0, span, columns] = value
                top, rest = split(value)
                solved[panel, part, 0, span, :] = top
                solved[panel, part, 1, span, :] = rest
            pass_down(panel, part)

    def form(tile):
        total = None
        for origin in range(ranks):
            term = lax.dot_general(
                gathered[origin, tile, 0],
                gathered[origin, tile, 1],
                (((1,), (1,)), ((), ())),
                preferred_element_type=jnp.float32,
            )
            total = term if total is None else total + term
        top, rest = split(total * scale[tile // 2, tile % 2])
        high[tile], low[tile] = top, rest

    def update(block):
        @pl.loop(0, chunks)
        def _(part):
            columns = pl.ds(pl.multiple_of(part * chunk, chunk), chunk)
            held[block, :, columns] = held[block, :, columns] - (
                product(2 * block, 0, part) + product(2 * block + 1, 1, part)
            )

    for tile in range(min(2, tiles)):
        for side in range(2):
            start_relay(side, tile, 0)

    @pl.when(row < 2)
    def _():
        prepare(row)

    loads[0].wait()

    @pl.when(row == 0)
    def _():
        solve(0)

    own_copy.wait()
    done = 0
    for slot in range(1, tiles + ranks - 1):
        for hop in range(ranks - 2, 0, -1):
            tile = slot - hop
            if 0 <= tile < tiles:
                for side in range(2):
                    wait_relay(side, tile, hop - 1)
                    start_relay(side, tile, hop)
        if slot + 1 < tiles:
            for side in range(2):
                start_relay(side, slot + 1, 0)
        tile = slot - (ranks - 1)
        if tile >= 0:
            for side in range(2):
                wait_relay(side, tile, ranks - 2)
            form(tile)
        if slot == ranks - 2:
            take_solution(0)
        if slot == ranks - 1:

            @pl.when(row == 1)
            def _():
                @pl.loop(0, chunks)
                def _(part):
                    columns = pl.ds(pl.multiple_of(part * chunk, chunk), chunk)
                    held[0, :, columns] = held[0, :, columns] - product(0, 0, part)

                solve(1)

        if slot == ranks + 1:
            take_solution(1)
        while slot >= ranks + 1 and done < blocks and 2 * done + 1 <= tile:
            if done == 0:

                @pl.when(row >= 2)
                def _():
                    update(0)

            else:
                loads[done].wait()
                update(done)
            stores[done].start()
            done += 1

    for side in range(2):
        for tile in range(tiles):
            for hop in range(ranks - 1):
                @pl.when(sends(side, hop))
                def _():
                    relay(side, tile, hop).wait_send()

    for panel in range(2):
        for part in range(chunks):
            pass_down(panel, part, start=False)
    for store in stores:
        store.wait()


def shards(right_sides, panel_diag, left_factor, right_factor, tile_scale, tile_rank):
    row_count, column_count = right_sides.shape
    size = panel_diag.shape[1]
    blocks = row_count // size
    tiles = 2 * blocks
    rows, ranks = lax.axis_size("row"), lax.axis_size("rhs")
    width = left_factor.shape[2]
    global_block = jnp.arange(blocks, dtype=jnp.int32) * rows + lax.axis_index("row")
    scale = jnp.where(
        global_block[:, None] > jnp.arange(2, dtype=jnp.int32)[None], tile_scale, 0.0
    )
    column = lax.axis_index("rhs") * width + jnp.arange(width, dtype=jnp.int32)
    used = column[None, None, None, :] < tile_rank[:, None, :, None]
    left = left_factor.reshape(blocks, size, 2, width)
    left = jnp.where(used, left, jnp.zeros((), left.dtype))
    right = right_factor.reshape(blocks, size, 2, width)
    factors = jnp.stack([left, right], axis=0).transpose(1, 3, 0, 2, 4)
    factors = factors.reshape(tiles, 2, size, width)
    chunk = min(256, column_count)
    chunks = column_count // chunk
    bits = rows.bit_length() - 1
    hops = ranks - 1
    out = pl.pallas_call(
        functools.partial(front_kernel, rows, ranks),
        out_shape=jax.ShapeDtypeStruct((blocks, size, column_count), jnp.float32),
        in_specs=[
            pl.BlockSpec(memory_space=pltpu.SMEM),
            pl.BlockSpec(memory_space=pl.ANY),
            pl.BlockSpec(memory_space=pltpu.VMEM),
            pl.BlockSpec(memory_space=pl.ANY),
        ],
        out_specs=pl.BlockSpec(memory_space=pl.ANY),
        scratch_shapes=[
            pltpu.VMEM((ranks, tiles, 2, size, width), jnp.bfloat16),
            pltpu.VMEM((blocks, size, column_count), jnp.float32),
            pltpu.VMEM((tiles, size, size), jnp.bfloat16),
            pltpu.VMEM((tiles, size, size), jnp.bfloat16),
            pltpu.VMEM((2, chunks, 2, size, chunk), jnp.bfloat16),
            pltpu.VMEM((size // BASE, BASE, BASE), jnp.float32),
            pltpu.SemaphoreType.DMA,
            pltpu.SemaphoreType.DMA((blocks,)),
            pltpu.SemaphoreType.DMA((blocks,)),
            pltpu.SemaphoreType.DMA((2, tiles, hops)),
            pltpu.SemaphoreType.DMA((2, tiles, hops)),
            pltpu.SemaphoreType.DMA((2, chunks, bits)),
            pltpu.SemaphoreType.DMA((2, chunks)),
        ],
        compiler_params=pltpu.CompilerParams(
            collective_id=0, has_side_effects=True, vmem_limit_bytes=60 * 1024 * 1024
        ),
    )(scale, right_sides.reshape(blocks, size, column_count), panel_diag, factors)
    return out.reshape(row_count, column_count)


def solution(mesh):
    placed = (
        P("row", "rhs"),
        P(),
        P("row", None, "rhs"),
        P("row", None, "rhs"),
        P("row", None),
        P("row", None),
    )
    return jax.shard_map(
        shards, mesh=mesh, in_specs=placed, out_specs=P("row", "rhs"), check_vma=False
    )
```

time: 294 us -> 178 us (0.61); the launches traced: 290 us -> 178 us
  Pallas kernels: 0 us -> 164 us
  waiting for transfers between devices: 97.7 us -> 0 us
  other arithmetic: 88.8 us -> 3.61 us
  matrix products: 55.9 us -> 0 us
  local copies, waits for them, and re-layouts: 32.3 us -> 10.2 us
  between operations: 15.1 us -> 0.04 us
    pallas_call x0 -> x1, Pallas kernels: none -> 164 us  [shards(): pl.pallas_call(functools.partial(front_kernel, rows, ranks), out_shape=ja...]
    another operation x4 -> x1, other arithmetic: 80.6 us -> 1.5 us  [shards(): factors = jnp.stack([left, right], axis=0).transpose(1, 3, 0, 2, 4)]
    all_gather x2 -> x0, waiting for transfers between devices: 49 us -> none  [the longest x1 49 us: shards(): lax.all_gather(right_factor, 'rhs', axis=2, tiled=True)]
    psum x2 -> x0, waiting for transfers between devices: 47.9 us -> none  [spread(): return lax.psum(kept, axis)]
    dot_general x6 -> x0, matrix products: 41.8 us -> none  [the longest x3 23.4 us: apply_panel(): jnp.einsum('lpr,lrn->lpn', left_blocks[chosen, :, panel_index, :], inner,...]
    another operation x27 -> x1, local copies, waits for them, and re-layouts: 16.1 us -> 0.14 us  [shards(): factors = jnp.stack([left, right], axis=0).transpose(1, 3, 0, 2, 4)]
    another operation x14 -> x0, matrix products: 14 us -> none  [solve_panel(): lax.linalg.triangular_solve(triangle, target, left_side=True, lower=True)]
    all_gather x1 -> x0, local copies, waits for them, and re-layouts: 5.09 us -> none  [shards(): lax.all_gather(left_factor, 'rhs', axis=2, tiled=True)]
  transfers between devices with their start and end apart: 4 -> 0, of which waited for: 3 -> 0; matrix products, arithmetic and copies ran while one was open for 44% -> 0% of each run, Pallas kernels for 0% -> 0%
where the time goes in v1:
time: 178 us
  Pallas kernels  164 us (92%)
  local copies, waits for them, and re-layouts  10.2 us (6%)
  other arithmetic  3.61 us (2%)
    pallas_call x1, Pallas kernels, shards(): pl.pallas_call(functools.partial(front_kernel, rows, ranks), out_shape=ja...  164 us
    unnamed x5, local copies, waits for them, and re-layouts  10.1 us

profile of v1, /device:TPU:7, one launch (start us, length us, event | category | flops | bytes accessed | tf_op | source)
XLA Modules:
  0.0 177.6 jit_solution(6517710804612730708)
XLA Ops:
  0.0 0.0 copy-start
  0.0 0.9 copy.7
  0.9 0.7 fusion.scale
  1.5 0.8 copy.8
  2.3 0.1 broadcast_compare_fusion
  2.4 1.4 copy_select_fusion
  3.7 0.0 copy-done
  3.7 0.1 copy.10
  3.9 1.5 pad_maximum_fusion
  5.4 163.7 %shard_map.64 = f32[4,512,1024]{2,1,0:T(8,128)} custom-call(f32[4,2]{1,0:T(4,128)} %fusion.scale, f32[4,512,1024]{2,1,0:T(8,128)} %bitcast.8, f32[2,512,512]{2,1,0:T(8,128)} %diag.1, bf16[8,2,512,128]{3,2,1,0:T(8,128)(2,1)} %bitcast.9), custom_call_target="tpu_custom_call" | custom-call | tf_op jit(solution)/shard_map/pallas_call | solution.py:279
  169.1 8.4 %copy.13 = f32[2048,1024]{1,0:T(8,128)} copy(f32[2048,1024]{1,0:T(8,128)} %bitcast.7) | data formatting | bytes 16777216
  (2 shorter events, 0.0 us)
Async XLA Ops:
  0.0 3.7 %copy-start = (bf16[2048,2,128]{2,1,0:T(2,128)(2,1)S(1)}, bf16[2048,2,128]{2,1,0:T(2,128)(2,1)}, u32[]{:S(2)}) copy-start(bf16[2048,2,128]{2,1,0:T(2,128)(2,1)} %param.9) | copy-start | bytes 3145732
